TPU v7x, 32 devices: a whole 2x2x4 slice. The times are simulated.
32 devices in a mesh: ctx: 4 (over z), head: 8 (over y, x, core).
Axes of the slice: x: 2, y: 2, z: 4, core: 2. Of those that a mesh axis runs over, the one named last changes fastest.
Arguments:
- queries: bfloat16 [2048, 2048], P('ctx', 'head'), may hold values from -24 to 24, as said below
- keys: bfloat16 [2048, 256], P('ctx'), may hold values from -24 to 24
- values: bfloat16 [2048, 256], P('ctx'), may hold values from -6 to 6
- out_grad: bfloat16 [2048, 2048], P('ctx', 'head'), may hold values from -6 to 6
- doc_start: int32 [2048], P('ctx'), may hold values from 0 to 2047, as said below
Outputs:
- attn_out: bfloat16 [2048, 2048], P('ctx', 'head')
- query_grad: bfloat16 [2048, 2048], P('ctx', 'head')
- key_grad: float32 [2048, 256], P('ctx', 'head')
- value_grad: float32 [2048, 256], P('ctx', 'head')
Inputs may be any that keep to these rules, and one draw needn't show every extreme that they name: Query and key entries lie within the range; in some draws a few queries are close to multiples of visible keys. doc_start[0] = 0; for i > 0 either doc_start[i] = i (a document begins) or doc_start[i] = doc_start[i - 1]. Documents may cross device boundaries. The last token begins a document of its own.
All inputs are finite; a program needn't handle non-finite values.
Results may differ from a plain program's by a relative error of at most 0.019.
Values may be sent and summed in bfloat16 or wider, within the bound.
No kernel may reach another device: no remote copies, remote signals or barrier semaphores. Data moves between devices by JAX's collectives and lax.ppermute only.
A program may use at most 64 MiB of HBM per device.

v0:
```python
import jax
import jax.numpy as jnp
from jax import lax
from jax.sharding import PartitionSpec as P

HEAD_DIM = 128
WINDOW = 1024


def from_behind(block, axis, distance):
    devices = range(lax.axis_size(axis))
    route = [(i - distance, i) for i in devices if i - distance in devices]
    return lax.ppermute(block, axis, route)


def from_partner(array, axis, stride):
    return lax.ppermute(array, axis, [(i, i ^ 1 << stride) for i in range(lax.axis_size(axis))])


def return_tails(grad_ext, key_reach, tok_rows, hop_count):
    owned_rows = grad_ext[:, key_reach:]
    offset = 0
    for distance in range(hop_count, 0, -1):
        row_count = min(tok_rows, key_reach - (distance - 1) * tok_rows)
        piece = grad_ext[:, offset : offset + row_count]
        offset = offset + row_count
        returned = from_behind(piece.astype(jnp.bfloat16), "ctx", -distance).astype(piece.dtype)
        owned_rows = owned_rows.at[:, tok_rows - row_count :].add(returned)
    return owned_rows


def group_sum(partial_value, head_index):
    head_width = partial_value.shape[2]
    quarter = head_width // 4
    partial_value = partial_value + from_partner(
        partial_value.astype(jnp.bfloat16), "head", 0
    ).astype(partial_value.dtype)
    partial_value = partial_value + from_partner(
        partial_value.astype(jnp.bfloat16), "head", 1
    ).astype(partial_value.dtype)
    return lax.dynamic_slice_in_dim(partial_value, head_index % 4 * quarter, quarter, 2)


def body(queries, keys, values, out_grad, doc_start):
    tok_rows = queries.shape[0]
    head_width = HEAD_DIM
    key_reach = WINDOW
    score_scale = HEAD_DIM ** (-0.5)
    head_index = lax.axis_index("head")
    kv_group = head_index // 4
    key_own = lax.dynamic_slice_in_dim(keys, kv_group * head_width, head_width, 1)
    value_own = lax.dynamic_slice_in_dim(values, kv_group * head_width, head_width, 1)
    stacked = jnp.stack([key_own, value_own])
    seq_offset = lax.axis_index("ctx") * tok_rows
    hop_count = -(-key_reach // tok_rows)
    pieces = []
    for distance in range(hop_count, 0, -1):
        pieces.append(from_behind(stacked, "ctx", distance))
    extended = jnp.concatenate(pieces + [stacked], axis=1)
    block_rows = min(512, tok_rows)
    query_heads = queries.reshape(tok_rows, 2, head_width)
    grad_heads = out_grad.reshape(tok_rows, 2, head_width)
    key_grad_ext = jnp.zeros((key_reach + tok_rows, head_width), jnp.float32)
    value_grad_ext = jnp.zeros((key_reach + tok_rows, head_width), jnp.float32)
    key_block = extended[0, 0 : block_rows + key_reach]
    value_block = extended[1, 0 : block_rows + key_reach]
    query_pos = seq_offset + 0 + jnp.arange(block_rows, dtype=jnp.int32)
    key_pos = seq_offset + 0 - key_reach + jnp.arange(block_rows + key_reach, dtype=jnp.int32)
    visible = (
        (key_pos[None, :] <= query_pos[:, None])
        & (key_pos[None, :] > query_pos[:, None] - key_reach)
        & (key_pos[None, :] >= doc_start[:, None])
    )
    scores = (
        jnp.einsum("qgd,kd->gqk", query_heads, key_block, preferred_element_type=jnp.float32)
        * score_scale
    )
    masked = jnp.where(visible[None], scores, -1e30)
    row_max = jnp.max(masked, axis=-1, keepdims=True)
    weights = jnp.where(visible[None], jnp.exp(masked - row_max), 0.0)
    prob_full = weights / jnp.sum(weights, axis=-1, keepdims=True)
    prob_round = prob_full.astype(jnp.bfloat16)
    attended = jnp.einsum(
        "gqk,kd->qgd", prob_round, value_block, preferred_element_type=jnp.float32
    ).astype(jnp.bfloat16)
    dprob = jnp.einsum("qgd,kd->gqk", grad_heads, value_block, preferred_element_type=jnp.float32)
    row_delta = jnp.transpose(
        jnp.sum(grad_heads.astype(jnp.float32) * attended.astype(jnp.float32), axis=-1), (1, 0)
    )
    dscore = (prob_full * (dprob - row_delta[:, :, None])).astype(jnp.bfloat16)
    qgrad_blocks = (
        jnp.einsum("gqk,kd->qgd", dscore, key_block, preferred_element_type=jnp.float32)
        * score_scale
    ).astype(jnp.bfloat16)
    key_part = (
        jnp.einsum("gqk,qgd->kd", dscore, query_heads, preferred_element_type=jnp.float32)
        * score_scale
    )
    value_part = jnp.einsum(
        "gqk,qgd->kd", prob_round, grad_heads, preferred_element_type=jnp.float32
    )
    key_grad_ext = key_grad_ext.at[0 : block_rows + key_reach].add(key_part)
    value_grad_ext = value_grad_ext.at[0 : block_rows + key_reach].add(value_part)
    attn_out = attended.reshape(tok_rows, 2 * head_width)
    query_grad = qgrad_blocks.reshape(tok_rows, 2 * head_width)
    grad_ext = jnp.stack([key_grad_ext, value_grad_ext])
    owned = group_sum(return_tails(grad_ext, key_reach, tok_rows, hop_count), head_index)
    return (attn_out, query_grad, owned[0], owned[1])


def solution(mesh):
    placed = (P("ctx", "head"), P("ctx", None), P("ctx", None), P("ctx", "head"), P("ctx"))
    return jax.shard_map(
        body,
        mesh=mesh,
        in_specs=placed,
        out_specs=(P("ctx", "head"), P("ctx", "head"), P("ctx", "head"), P("ctx", "head")),
        check_vma=False,
    )
```

profile of v0, /device:TPU:8, one launch (start us, length us, event | category | flops | bytes accessed | tf_op | source)
XLA Modules:
  0.0 66.7 jit_solution(8524694277647806956)
XLA Ops:
  0.7 1.0 %dynamic-slice_bitcast_fusion = (bf16[1,512,128]{2,1,0:T(8,128)(2,1)S(1)}, bf16[1,512,128]{2,1,0:T(8,128)(2,1)S(1)}) fusion(bf16[512,256]{1,0:T(8,128)(2,1)} %param.23, s32[]{:T(128)S(6)} %select_n.26, bf16[512,256]{1,0:T(8,128)(2,1)} %param.22), kind=kLoop, calls=%fused_computation.36 | loop fusion | bytes 524292 | tf_op jit(solution)/shard_map/stack | solution.py:53
  1.7 3.5 %collective-permute-start.1 = (bf16[2,512,128]{2,1,0:T(8,128)(2,1)S(1)}, bf16[2,512,128]{2,1,0:T(8,128)(2,1)S(1)}, u32[]{:S(2)}, u32[]{:S(2)}) collective-permute-start(bf16[2,512,128]{2,1,0:T(8,128)(2,1)S(1)} %pad_maximum_fusion.1), channel_id=1, source_target_pairs={{0,8},{8,16},{16,24},{1,9},{9,17},{17,25},{2,10},{10,18},{18,26},{... | collective-permute-start | bytes 786440 | tf_op jit(solution)/shard_map/ppermute | solution.py:13
  5.2 2.3 %collective-permute-start = (bf16[2,512,128]{2,1,0:T(8,128)(2,1)S(1)}, bf16[2,512,128]{2,1,0:T(8,128)(2,1)S(1)}, u32[]{:S(2)}, u32[]{:S(2)}) collective-permute-start(bf16[2,512,128]{2,1,0:T(8,128)(2,1)S(1)} %pad_maximum_fusion.1), channel_id=1, source_target_pairs={{0,16},{8,24},{1,17},{9,25},{2,18},{10,26},{3,19},{11,27},{4,20},{... | collective-permute-start | bytes 786440 | tf_op jit(solution)/shard_map/ppermute | solution.py:13
  7.5 1.1 %copy.12 = bf16[512,256]{0,1:T(8,128)(2,1)S(1)} copy(bf16[512,256]{1,0:T(8,128)(2,1)} %param.24) | data formatting | bytes 524288 | tf_op args[3]
  8.6 1.1 %copy.30 = bf16[512,256]{0,1:T(8,128)(2,1)S(1)} copy(bf16[512,256]{1,0:T(8,128)(2,1)} %param.21) | data formatting | bytes 524288 | tf_op jit(solution)/shard_map/reshape | solution.py:61
  9.7 0.0 copy-start.7
  9.7 1.9 %compare_and_fusion = pred[512,1536]{0,1:T(8,128)(4,1)S(1)} fusion(s32[512]{0:T(512)} %param.25, s32[512]{0:T(512)S(1)} %get-tuple-element.99, s32[512]{0:T(512)S(1)} %get-tuple-element.98, s32[1536]{0:T(1024)S(1)} %iota_add_fusion), kind=kLoop, calls=%fused_computation.11 | loop fusion | flops 3932160 | bytes 798720 | tf_op jit(solution)/shard_map/and | solution.py:70
  11.6 5.9 %collective-permute-done.1 = bf16[2,512,128]{2,1,0:T(8,128)(2,1)S(1)} collective-permute-done((bf16[2,512,128]{2,1,0:T(8,128)(2,1)S(1)}, bf16[2,512,128]{2,1,0:T(8,128)(2,1)S(1)}, u32[]{:S(2)}, u32[]{:S(2)}) %collective-permute-start.1) | collective-permute-done | bytes 262176 | tf_op jit(solution)/shard_map/ppermute | solution.py:13
  17.5 4.5 %collective-permute-done = bf16[2,512,128]{2,1,0:T(8,128)(2,1)S(1)} collective-permute-done((bf16[2,512,128]{2,1,0:T(8,128)(2,1)S(1)}, bf16[2,512,128]{2,1,0:T(8,128)(2,1)S(1)}, u32[]{:S(2)}, u32[]{:S(2)}) %collective-permute-start) | collective-permute-done | bytes 262176 | tf_op jit(solution)/shard_map/ppermute | solution.py:13
  22.0 0.1 maximum_maximum_fusion
  22.0 0.0 copy-start.2
  22.0 4.9 %fusion.23 = (f32[2,512]{1,0:T(2,128)S(1)}, f32[2,512,1536]{1,2,0:T(8,128)}) fusion(pred[512,1536]{0,1:T(8,128)(4,1)S(1)} %compare_and_fusion, bf16[512,2,128]{0,2,1:T(8,128)(2,1)S(1)} %bitcast.78, bf16[2,1536,128]{2,1,0:T(8,128)(2,1)S(1)} %maximum_maximum_fusion), kind=kOutput, calls=%fused_computation.48 | convolution fusion | flops 410519040 | bytes 8523776 | tf_op jit(solution)/shard_map/sub | solution.py:80
  26.9 0.0 copy-done.7
  26.9 0.0 slice-start
  26.9 3.8 %fusion.7 = bf16[2,512,1536]{1,2,0:T(8,128)(2,1)S(1)} fusion(f32[2,512,1536]{1,2,0:T(8,128)} %get-tuple-element.95, f32[2,512]{1,0:T(2,128)S(1)} %get-tuple-element.94), kind=kLoop, calls=%fused_computation.12 | loop fusion | flops 3145728 | bytes 9441280 | tf_op jit(solution)/shard_map/convert_element_type | solution.py:82
  30.7 0.0 copy-done.2
  30.7 0.0 slice-start.1
  30.8 1.3 %multiply_reduce_fusion = (f32[512,2]{0,1:T(2,128)S(1)}, bf16[128,2,512]{2,0,1:T(8,128)(2,1)}) fusion(bf16[512,256]{0,1:T(8,128)(2,1)S(1)} %copy.12, bf16[2,512,1536]{1,2,0:T(8,128)(2,1)S(1)} %fusion.7, bf16[2,1536,128]{2,1,0:T(8,128)(2,1)S(1)} %maximum_maximum_fusion), kind=kOutput, calls=%fused_computation.30 | convolution fusion | flops 403307520 | bytes 4067328 | tf_op jit(solution)/shard_map/gqk,kd->qgd/dot_general | solution.py:83
  32.1 0.0 copy-start.3
  32.1 1.1 %convolution_bitcast_fusion = f32[1,1536,128]{1,2,0:T(8,128)S(1)} fusion(bf16[2,512,1536]{1,2,0:T(8,128)(2,1)S(1)} %fusion.7, bf16[512,2,128]{0,2,1:T(8,128)(2,1)S(1)} %bitcast.75), kind=kOutput, calls=%fused_computation.13 | convolution fusion | flops 402653184 | bytes 4194304 | tf_op jit(solution)/shard_map/gqk,qgd->kd/dot_general | solution.py:99
  33.2 0.0 copy-start
  33.2 0.0 slice-done
  33.2 0.0 slice-done.1
  33.2 0.0 copy-done.3
  33.3 0.0 copy-start.8
  33.3 1.0 %fusion.2 = bf16[2,512,1536]{1,2,0:T(8,128)(2,1)S(1)} fusion(bf16[512,2,128]{0,2,1:T(8,128)(2,1)S(1)} %bitcast.76, f32[2,512]{1,0:T(2,128)S(1)} %bitcast.81, f32[2,512,1536]{1,2,0:T(8,128)S(1)} %bitcast.74, f32[2,512]{1,0:T(2,128)S(1)} %get-tuple-element.94, bf16[2,1536,128]{2,1,0:T(8,128)(2,1)S(1)} %copy-done.3), kind=kOutput, calls=%fused_computation.3 | convolution fusion | flops 408944640 | bytes 10100736 | tf_op jit(solution)/shard_map/qgd,kd->gqk/dot_general | solution.py:86
  34.3 0.2 copy-done.8
  34.4 1.1 %fusion.9 = f32[1,1536,128]{1,2,0:T(8,128)S(1)} fusion(bf16[2,512,1536]{1,2,0:T(8,128)(2,1)S(1)} %fusion.2, bf16[512,2,128]{0,2,1:T(8,128)(2,1)S(1)} %bitcast.79), kind=kOutput, calls=%fused_computation.16 | convolution fusion | flops 402849792 | bytes 4194304 | tf_op jit(solution)/shard_map/gqk,qgd->kd/dot_general | solution.py:96
  35.6 0.0 copy-start.1
  35.6 0.1 fusion.10
  35.7 1.3 %collective-permute-start.2 = (bf16[2,512,128]{1,2,0:T(8,128)(2,1)S(1)}, bf16[2,512,128]{1,2,0:T(8,128)(2,1)S(1)}, u32[]{:S(2)}, u32[]{:S(2)}) collective-permute-start(bf16[2,512,128]{1,2,0:T(8,128)(2,1)S(1)} %get-tuple-element.90), channel_id=1, source_target_pairs={{16,0},{24,8},{17,1},{25,9},{18,2},{26,10},{19,3},{27,11},{20,4},{... | collective-permute-start | bytes 786440 | tf_op jit(solution)/shard_map/ppermute | solution.py:13
  37.0 1.9 %collective-permute-start.3 = (bf16[2,512,128]{1,2,0:T(8,128)(2,1)S(1)}, bf16[2,512,128]{1,2,0:T(8,128)(2,1)S(1)}, u32[]{:S(2)}, u32[]{:S(2)}) collective-permute-start(bf16[2,512,128]{1,2,0:T(8,128)(2,1)S(1)} %get-tuple-element.91), channel_id=1, source_target_pairs={{8,0},{16,8},{24,16},{9,1},{17,9},{25,17},{10,2},{18,10},{26,18},{... | collective-permute-start | bytes 786440 | tf_op jit(solution)/shard_map/ppermute | solution.py:13
  39.0 8.8 %collective-permute-done.2 = bf16[2,512,128]{1,2,0:T(8,128)(2,1)S(1)} collective-permute-done((bf16[2,512,128]{1,2,0:T(8,128)(2,1)S(1)}, bf16[2,512,128]{1,2,0:T(8,128)(2,1)S(1)}, u32[]{:S(2)}, u32[]{:S(2)}) %collective-permute-start.2) | collective-permute-done | bytes 262176 | tf_op jit(solution)/shard_map/ppermute | solution.py:13
  47.8 3.6 %collective-permute-done.3 = bf16[2,512,128]{1,2,0:T(8,128)(2,1)S(1)} collective-permute-done((bf16[2,512,128]{1,2,0:T(8,128)(2,1)S(1)}, bf16[2,512,128]{1,2,0:T(8,128)(2,1)S(1)}, u32[]{:S(2)}, u32[]{:S(2)}) %collective-permute-start.3) | collective-permute-done | bytes 262176 | tf_op jit(solution)/shard_map/ppermute | solution.py:13
  51.5 0.0 copy-done
  51.5 0.0 copy-start.5
  51.5 0.8 %fusion.20 = bf16[2,512,128]{1,2,0:T(8,128)(2,1)} fusion(bf16[2,512,128]{1,2,0:T(8,128)(2,1)S(1)} %collective-permute-done.3, bf16[2,512,128]{1,2,0:T(8,128)(2,1)S(1)} %collective-permute-done.2, f32[1,1536,128]{1,2,0:T(8,128)S(1)} %convolution_bitcast_fusion, f32[1,1536,128]{1,2,0:T(8,128)S(1)} %fusion.9), kind=kLoop, calls=%fused_computation.45 | loop fusion | flops 786432 | bytes 2359296 | tf_op jit(solution)/shard_map/convert_element_type | solution.py:36
  52.3 0.0 copy-done.1
  52.3 0.0 copy-done.5
  52.3 0.0 collective-permute-start.4
  52.3 0.0 copy-start.4
  52.3 1.8 %collective-permute-done.4 = bf16[2,512,128]{1,2,0:T(8,128)(2,1)} collective-permute-done((bf16[2,512,128]{1,2,0:T(8,128)(2,1)}, bf16[2,512,128]{1,2,0:T(8,128)(2,1)}, u32[]{:S(2)}, u32[]{:S(2)}) %collective-permute-start.4) | collective-permute-done | bytes 262176 | tf_op jit(solution)/shard_map/ppermute | solution.py:17
  54.2 2.2 %fusion.21 = (bf16[2,512,128]{1,2,0:T(8,128)(2,1)}, f32[2,512,128]{1,2,0:T(8,128)}) fusion(bf16[2,512,128]{1,2,0:T(8,128)(2,1)} %collective-permute-done.4, bf16[2,512,128]{1,2,0:T(8,128)(2,1)} %copy-done.5, bf16[2,512,128]{1,2,0:T(8,128)(2,1)S(1)} %collective-permute-done.2, f32[1,1536,128]{1,2,0:T(8,128)} %copy-done, f32[1,1536,128]{1,2,0:T(8,128)} %copy-done.1), kind=kLoop, calls=%fused_computation.46 | loop fusion | flops 1048576 | bytes 3145728 | tf_op jit(solution)/shard_map/convert_element_type | solution.py:39
  56.4 0.0 copy-start.6
  56.4 1.5 %collective-permute-start.5 = (bf16[2,512,128]{1,2,0:T(8,128)(2,1)}, bf16[2,512,128]{1,2,0:T(8,128)(2,1)}, u32[]{:S(2)}, u32[]{:S(2)}) collective-permute-start(bf16[2,512,128]{1,2,0:T(8,128)(2,1)} %get-tuple-element.88), channel_id=1, source_target_pairs={{0,2},{1,3},{2,0},{3,1},{4,6},{5,7},{6,4},{7,5},{8,10},{9,11},{10,... | collective-permute-start | bytes 786440 | tf_op jit(solution)/shard_map/ppermute | solution.py:17
  57.9 0.0 copy-done.4
  57.9 1.3 %fusion.11 = bf16[128,2,512]{2,0,1:T(8,128)(2,1)} fusion(bf16[2,512,1536]{1,2,0:T(8,128)(2,1)S(1)} %fusion.2, bf16[2,1536,128]{2,1,0:T(8,128)(2,1)S(1)} %copy-done.4), kind=kOutput, calls=%fused_computation.22 | convolution fusion | flops 402915328 | bytes 3801088 | tf_op jit(solution)/shard_map/gqk,kd->qgd/dot_general | solution.py:92
  59.2 1.8 %copy.20 = bf16[512,256]{1,0:T(8,128)(2,1)} copy(bf16[512,256]{0,1:T(8,128)(2,1)} %bitcast.80) | data formatting | bytes 524288
  61.0 0.0 copy-done.6
  61.0 0.8 %copy.19 = bf16[512,256]{1,0:T(8,128)(2,1)} copy(bf16[512,256]{0,1:T(8,128)(2,1)S(1)} %bitcast.77) | data formatting | bytes 524288
  61.8 3.3 %collective-permute-done.5 = bf16[2,512,128]{1,2,0:T(8,128)(2,1)} collective-permute-done((bf16[2,512,128]{1,2,0:T(8,128)(2,1)}, bf16[2,512,128]{1,2,0:T(8,128)(2,1)}, u32[]{:S(2)}, u32[]{:S(2)}) %collective-permute-start.5) | collective-permute-done | bytes 262176 | tf_op jit(solution)/shard_map/ppermute | solution.py:17
  65.1 0.9 %dynamic-slice_add_fusion = f32[2,512,32]{1,2,0:T(8,128)S(1)} fusion(f32[2,512,128]{1,2,0:T(8,128)} %get-tuple-element.89, s32[]{:T(128)S(6)} %select_n.30, bf16[2,512,128]{1,2,0:T(8,128)(2,1)} %collective-permute-done.5), kind=kLoop, calls=%fused_computation.35 | loop fusion | flops 65536 | bytes 327684 | tf_op jit(solution)/shard_map/add | solution.py:38
  66.0 0.7 slice_bitcast_fusion.10
  (5 shorter events, 0.1 us)
Async XLA Ops:
  1.7 15.8 %collective-permute-start.1 = (bf16[2,512,128]{2,1,0:T(8,128)(2,1)S(1)}, bf16[2,512,128]{2,1,0:T(8,128)(2,1)S(1)}, u32[]{:S(2)}, u32[]{:S(2)}) collective-permute-start(bf16[2,512,128]{2,1,0:T(8,128)(2,1)S(1)} %pad_maximum_fusion.1), channel_id=1, source_target_pairs={{0,8},{8,16},{16,24},{1,9},{9,17},{17,25},{2,10},{10,18},{18,26},{... | collective-permute-start | bytes 786440 | tf_op jit(solution)/shard_map/ppermute | solution.py:13
  5.2 16.8 %collective-permute-start = (bf16[2,512,128]{2,1,0:T(8,128)(2,1)S(1)}, bf16[2,512,128]{2,1,0:T(8,128)(2,1)S(1)}, u32[]{:S(2)}, u32[]{:S(2)}) collective-permute-start(bf16[2,512,128]{2,1,0:T(8,128)(2,1)S(1)} %pad_maximum_fusion.1), channel_id=1, source_target_pairs={{0,16},{8,24},{1,17},{9,25},{2,18},{10,26},{3,19},{11,27},{4,20},{... | collective-permute-start | bytes 786440 | tf_op jit(solution)/shard_map/ppermute | solution.py:13
  9.7 17.2 %copy-start.7 = (bf16[512,256]{0,1:T(8,128)(2,1)}, bf16[512,256]{0,1:T(8,128)(2,1)S(1)}, u32[]{:S(2)}) copy-start(bf16[512,256]{0,1:T(8,128)(2,1)S(1)} %copy.30) | copy-start | bytes 786436
  22.0 8.7 %copy-start.2 = (bf16[2,1536,128]{2,1,0:T(8,128)(2,1)}, bf16[2,1536,128]{2,1,0:T(8,128)(2,1)S(1)}, u32[]{:S(2)}) copy-start(bf16[2,1536,128]{2,1,0:T(8,128)(2,1)S(1)} %maximum_maximum_fusion) | copy-start | bytes 2359300
  26.9 6.3 %slice-start = ((s8[6291456]{0:T(1024)(128)(4,1)}), s8[4194304]{0:T(1024)(128)(4,1)S(1)}, s32[]{:S(2)}) async-start(s8[6291456]{0:T(1024)(128)(4,1)} %bitcast.73), calls=%async_computation | async-start | bytes 8388608
  30.7 2.5 %slice-start.1 = ((s8[6291456]{0:T(1024)(128)(4,1)}), s8[2097152]{0:T(1024)(128)(4,1)S(1)}, s32[]{:S(2)}) async-start(s8[6291456]{0:T(1024)(128)(4,1)} %bitcast.73), calls=%async_computation.1 | async-start | bytes 4194304
  32.1 1.2 %copy-start.3 = (bf16[2,1536,128]{2,1,0:T(8,128)(2,1)S(1)}, bf16[2,1536,128]{2,1,0:T(8,128)(2,1)}, u32[]{:S(2)}) copy-start(bf16[2,1536,128]{2,1,0:T(8,128)(2,1)} %copy-done.2) | copy-start | bytes 2359300
  33.2 18.2 %copy-start = (f32[1,1536,128]{1,2,0:T(8,128)}, f32[1,1536,128]{1,2,0:T(8,128)S(1)}, u32[]{:S(2)}) copy-start(f32[1,1536,128]{1,2,0:T(8,128)S(1)} %convolution_bitcast_fusion) | copy-start | bytes 2359300
  33.3 1.2 %copy-start.8 = (bf16[512,256]{0,1:T(8,128)(2,1)S(1)}, bf16[512,256]{0,1:T(8,128)(2,1)}, u32[]{:S(2)}) copy-start(bf16[512,256]{0,1:T(8,128)(2,1)} %copy-done.7) | copy-start | bytes 786436
  35.6 16.7 %copy-start.1 = (f32[1,1536,128]{1,2,0:T(8,128)}, f32[1,1536,128]{1,2,0:T(8,128)S(1)}, u32[]{:S(2)}) copy-start(f32[1,1536,128]{1,2,0:T(8,128)S(1)} %fusion.9) | copy-start | bytes 2359300
  35.7 12.1 %collective-permute-start.2 = (bf16[2,512,128]{1,2,0:T(8,128)(2,1)S(1)}, bf16[2,512,128]{1,2,0:T(8,128)(2,1)S(1)}, u32[]{:S(2)}, u32[]{:S(2)}) collective-permute-start(bf16[2,512,128]{1,2,0:T(8,128)(2,1)S(1)} %get-tuple-element.90), channel_id=1, source_target_pairs={{16,0},{24,8},{17,1},{25,9},{18,2},{26,10},{19,3},{27,11},{20,4},{... | collective-permute-start | bytes 786440 | tf_op jit(solution)/shard_map/ppermute | solution.py:13
  37.0 14.4 %collective-permute-start.3 = (bf16[2,512,128]{1,2,0:T(8,128)(2,1)S(1)}, bf16[2,512,128]{1,2,0:T(8,128)(2,1)S(1)}, u32[]{:S(2)}, u32[]{:S(2)}) collective-permute-start(bf16[2,512,128]{1,2,0:T(8,128)(2,1)S(1)} %get-tuple-element.91), channel_id=1, source_target_pairs={{8,0},{16,8},{24,16},{9,1},{17,9},{25,17},{10,2},{18,10},{26,18},{... | collective-permute-start | bytes 786440 | tf_op jit(solution)/shard_map/ppermute | solution.py:13
  51.5 0.8 %copy-start.5 = (bf16[2,512,128]{1,2,0:T(8,128)(2,1)}, bf16[2,512,128]{1,2,0:T(8,128)(2,1)S(1)}, u32[]{:S(2)}) copy-start(bf16[2,512,128]{1,2,0:T(8,128)(2,1)S(1)} %collective-permute-done.3) | copy-start | bytes 786436
  52.3 1.9 %collective-permute-start.4 = (bf16[2,512,128]{1,2,0:T(8,128)(2,1)}, bf16[2,512,128]{1,2,0:T(8,128)(2,1)}, u32[]{:S(2)}, u32[]{:S(2)}) collective-permute-start(bf16[2,512,128]{1,2,0:T(8,128)(2,1)} %fusion.20), channel_id=1, source_target_pairs={{0,1},{1,0},{2,3},{3,2},{4,5},{5,4},{6,7},{7,6},{8,9},{9,8},{10,11... | collective-permute-start | bytes 786440 | tf_op jit(solution)/shard_map/ppermute | solution.py:17
  52.3 5.6 %copy-start.4 = (bf16[2,1536,128]{2,1,0:T(8,128)(2,1)S(1)}, bf16[2,1536,128]{2,1,0:T(8,128)(2,1)}, u32[]{:S(2)}) copy-start(bf16[2,1536,128]{2,1,0:T(8,128)(2,1)} %copy-done.2) | copy-start | bytes 2359300
  56.4 4.6 %copy-start.6 = (bf16[128,2,512]{2,0,1:T(8,128)(2,1)S(1)}, bf16[128,2,512]{2,0,1:T(8,128)(2,1)}, u32[]{:S(2)}) copy-start(bf16[128,2,512]{2,0,1:T(8,128)(2,1)} %get-tuple-element.97) | copy-start | bytes 786436
  56.4 8.7 %collective-permute-start.5 = (bf16[2,512,128]{1,2,0:T(8,128)(2,1)}, bf16[2,512,128]{1,2,0:T(8,128)(2,1)}, u32[]{:S(2)}, u32[]{:S(2)}) collective-permute-start(bf16[2,512,128]{1,2,0:T(8,128)(2,1)} %get-tuple-element.88), channel_id=1, source_target_pairs={{0,2},{1,3},{2,0},{3,1},{4,6},{5,7},{6,4},{7,5},{8,10},{9,11},{10,... | collective-permute-start | bytes 786440 | tf_op jit(solution)/shard_map/ppermute | solution.py:17
where the time goes:
time: 67.1 us; the launch traced here: 66.7 us
  waiting for transfers between devices  27.9 us (42%)
  matrix products  10.7 us (16%)
  starting transfers between devices  10.5 us (16%)
  other arithmetic  9.88 us (15%)
  local copies, waits for them, and re-layouts  6.73 us (10%)
  between operations  0.88 us (1%)
    ppermute x4, waiting for transfers between devices, from_behind(): return lax.ppermute(block, axis, route)  22.8 us
    ppermute x4, starting transfers between devices, from_behind(): return lax.ppermute(block, axis, route)  9.01 us
    ppermute x2, waiting for transfers between devices, from_partner(): lax.ppermute(array, axis, [(i, i ^ 1 << stride) for i in range(lax.axis_s...  5.11 us
    sub x1, matrix products, body(): weights = jnp.where(visible[None], jnp.exp(masked - row_max), 0.0)  4.86 us
    unnamed x25, local copies, waits for them, and re-layouts  3.95 us
    convert_element_type x1, other arithmetic, body(): prob_round = prob_full.astype(jnp.bfloat16)  3.84 us
    convert_element_type x2, other arithmetic, group_sum(): partial_value.astype(jnp.bfloat16)  3.06 us
    and x1, other arithmetic, body(): (key_pos[None, :] <= query_pos[:, None]) & (key_pos[None, :] > query_pos[...  1.87 us
  transfers between devices with their start and end apart: 6, of which 6 were waited for; matrix products, arithmetic and copies ran while one was open for 12% of the time, Pallas kernels for 0%

commit v1 on v0

v1 whole, which is shorter than its diff:
```python
import functools
import math

import jax
import jax.numpy as jnp
from jax import lax
from jax.experimental import pallas as pl
from jax.experimental.pallas import tpu as pltpu
from jax.sharding import PartitionSpec as P

HEAD_DIM = 128
WINDOW = 1024
GROUP = 4
SCALE = HEAD_DIM**-0.5
EXP2_SCALE = SCALE * math.log2(math.e)
HIDDEN = -1e30
SAFE_SUM = 2.0**64
F32 = jnp.float32
BF16 = jnp.bfloat16

NN = (((1,), (0,)), ((), ()))
NT = (((1,), (1,)), ((), ()))


def dot(a, b, dims):
    return lax.dot_general(a, b, dims, preferred_element_type=F32)


def tile_of(tok):
    return min(256, tok)


def col_blocks(tok, heads):
    tile = tile_of(tok)
    return [
        (t * tile, h, (t * heads + h) * tile) for t in range(tok // tile) for h in range(heads)
    ]


def wide_blocks(tok, heads):
    tile = tile_of(tok)
    return [(t * tile, slice(t * heads * tile, (t + 1) * heads * tile)) for t in range(tok // tile)]


def place_of(q0, h, tile):
    return slice(q0, q0 + tile), slice(h * HEAD_DIM, (h + 1) * HEAD_DIM)


def first_visible(doc_ref, q0, tile):
    start = lax.axis_index("ctx") * doc_ref.shape[1]
    query = q0 + lax.broadcasted_iota(jnp.int32, (1, tile), 1)
    return jnp.maximum(doc_ref[:, q0 : q0 + tile] - start, query - (WINDOW - 1))


def with_ones(vt):
    return jnp.concatenate([vt, jnp.ones((16, vt.shape[1]), BF16)], axis=0)


def weigh(vt_ones, eb):
    both = dot(vt_ones, eb, NN)
    return both[:HEAD_DIM], both[HEAD_DIM : HEAD_DIM + 1]


def pack_kernel(keys_hbm, values_hbm, half_ref, quarter_ref, sems):
    last = lax.axis_size("ctx") - 1
    head = lax.axis_index("head")
    tok = half_ref.shape[0]
    lanes = pl.ds(pl.multiple_of(head // GROUP * HEAD_DIM, HEAD_DIM), HEAD_DIM)
    rows = pl.ds(pl.multiple_of(head // 2 % 2 * (tok // 2), tok // 2), tok // 2)
    for odd, source in enumerate((keys_hbm, values_hbm)):

        @pl.when((lax.axis_index("ctx") + 2 <= last) & (head % 2 == odd))
        def _():
            copies = [
                pltpu.make_async_copy(source.at[rows, lanes], quarter_ref, sems.at[0]),
                pltpu.make_async_copy(source.at[:, lanes], half_ref, sems.at[1]),
            ]
            for copy in copies:
                copy.start()
            for copy in copies:
                copy.wait()


def late_pack_kernel(keys_hbm, values_hbm, _, half_ref, sem):
    last = lax.axis_size("ctx") - 1
    head = lax.axis_index("head")
    lanes = pl.ds(pl.multiple_of(head // GROUP * HEAD_DIM, HEAD_DIM), HEAD_DIM)
    for odd, source in enumerate((keys_hbm, values_hbm)):

        @pl.when((lax.axis_index("ctx") + 1 == last) & (head % 2 == odd))
        def _():
            copy = pltpu.make_async_copy(source.at[:, lanes], half_ref, sem)
            copy.start()
            copy.wait()


def beside_ones(rows):
    return jnp.concatenate([rows, jnp.ones((rows.shape[0], HEAD_DIM), BF16)], axis=1)


def less(columns, row):
    high = row.astype(BF16).astype(F32)
    middle = (row - high).astype(BF16).astype(F32)
    low = row - high - middle
    which = lax.broadcasted_iota(jnp.int32, (16, row.shape[1]), 0)
    block = jnp.where(which == 0, high, jnp.where(which == 1, middle, low))
    block = jnp.where(which < 3, -block, 0.0).astype(BF16)
    rest = jnp.zeros((HEAD_DIM - 16, row.shape[1]), BF16)
    return jnp.concatenate([columns, block, rest], axis=0)


def causal_kernel(bias_ref):
    key = lax.broadcasted_iota(jnp.int32, bias_ref.shape, 0)
    query = lax.broadcasted_iota(jnp.int32, bias_ref.shape, 1)
    bias_ref[...] = jnp.where(key <= query, 0.0, HIDDEN)


def own_kernel(
    tok, heads, causal_ref, doc_ref, q_ref, keys_ref, do_ref, values_ref,
    e_ref, dp_ref, o_ref, stat_ref, qt_ref, dot_ref, kt_ref, s_ref,
):
    tile = tile_of(tok)
    group = lax.axis_index("head") // GROUP
    lanes = pl.ds(pl.multiple_of(group * HEAD_DIM, HEAD_DIM), HEAD_DIM)
    k = keys_ref[:, lanes]
    v = values_ref[:, lanes]
    for q0, h, c0 in col_blocks(tok, heads):
        place = place_of(q0, h, tile)
        qt_ref[:, c0 : c0 + tile] = q_ref[place].T
        dot_ref[:, c0 : c0 + tile] = do_ref[place].T
    wide = wide_blocks(tok, heads)
    for q0, cols in wide:
        rows = q0 + tile
        first = first_visible(doc_ref, q0, tile)
        key = lax.broadcasted_iota(jnp.int32, (tile, tile), 0)
        bias = [jnp.where(key + r0 >= first, 0.0, HIDDEN) for r0 in range(0, q0, tile)]
        bias.append(jnp.where(key + q0 >= first, causal_ref[...], HIDDEN))
        bias = jnp.concatenate(bias, axis=0)
        s = dot(k[:rows], qt_ref[:, cols], NN) + jnp.concatenate([bias] * heads, axis=1)
        s_ref[0:rows, cols] = s
        stat_ref[0:1, cols] = jnp.max(s, axis=0, keepdims=True)
    kt_ref[...] = k.T
    vt = with_ones(v.T)
    for q0, cols in wide:
        rows = q0 + tile
        eb = jnp.exp2((s_ref[0:rows, cols] - stat_ref[0:1, cols]) * EXP2_SCALE).astype(BF16)
        e_ref[0:rows, cols] = eb
        o_ref[:, cols], stat_ref[1:2, cols] = weigh(vt[:, :rows], eb)
        dp_ref[0:rows, cols] = dot(v[:rows], dot_ref[:, cols], NN)


def gather_block(pieces):
    member = lax.axis_index("head") % GROUP
    odd, high = member % 2 == 1, member // 2 == 1
    if len(pieces) == 2:
        mine, other = pieces[0][...], pieces[1][...]
    else:
        mine, mine_x, other, other_x = [p[...] for p in pieces]
        mine = [jnp.where(high, mine_x, mine), jnp.where(high, mine, mine_x)]
        other = [jnp.where(high, other_x, other), jnp.where(high, other, other_x)]
        mine, other = jnp.concatenate(mine, axis=0), jnp.concatenate(other, axis=0)
    return jnp.where(odd, other, mine), jnp.where(odd, mine, other)


def write_part(send_ref, keep_ref, g_ref, which):
    part = HEAD_DIM // GROUP
    member = lax.axis_index("head") % GROUP
    odd, high = member % 2, member // 2
    for far in range(2):
        x = high if far == 0 else 1 - high
        mine = pl.ds(pl.multiple_of((2 * x + odd) * part, part), part)
        theirs = pl.ds(pl.multiple_of((2 * x + 1 - odd) * part, part), part)
        keep_ref[far, which] = g_ref[which, mine, :]
        send_ref[far, which] = g_ref[which, theirs, :].astype(BF16)


def write_parts(send_ref, keep_ref, g_ref):
    for which in range(2):
        write_part(send_ref, keep_ref, g_ref, which)


def exists(distance):
    return lax.axis_index("ctx") >= distance


def weights_of(k, vt, bias, m, queries_t, s_ref, e_ref, exact):
    if exact:
        s = dot(k[:, :HEAD_DIM], queries_t, NN) + bias
        s_ref[...] = s
        m = jnp.maximum(m, jnp.max(s, axis=0, keepdims=True))
        s = s_ref[...] - m
    else:
        s = dot(k, less(queries_t, m), NN) + bias
    eb = jnp.exp2(s * EXP2_SCALE).astype(BF16)
    e_ref[...] = eb
    o, total = weigh(vt, eb)
    return m, o, total


def twice(run):
    totals = run(False)
    highest = functools.reduce(jnp.maximum, [jnp.max(total) for total in totals])

    @pl.when(jnp.logical_not(highest <= SAFE_SUM))
    def _():
        run(True)


def mask_kernel(tok, doc_ref, near_ref, far_ref):
    tile = tile_of(tok)
    far = far_ref.shape[0]
    for q0 in range(0, tok, tile):
        first = first_visible(doc_ref, q0, tile)
        cols = slice(q0, q0 + tile)
        key = lax.broadcasted_iota(jnp.int32, (tok, tile), 0) - tok
        near_ref[:, cols] = jnp.where(key >= first, 0.0, HIDDEN)
        key = (q0 - far - tok) + lax.broadcasted_iota(jnp.int32, (far - q0, tile), 0)
        far_ref[q0:, cols] = jnp.where(key >= first, 0.0, HIDDEN)


def near_kernel(
    tok, heads, bias_ref, o_own, stat_own, qt_ref, mine_ref, other_ref,
    e_ref, o_ref, stat_ref, k_ref, v_ref, s_ref,
):
    tile = tile_of(tok)

    def run(exact):
        k, v = gather_block((mine_ref, other_ref))
        k_ref[...] = k
        v_ref[...] = v
        k = beside_ones(k)
        vt = with_ones(v.T)
        totals = []
        wide = [bias_ref[:, q0 : q0 + tile] for q0, _, _ in col_blocks(tok, heads)]
        m_own = stat_own[0:1, :]
        m, o, total = weights_of(
            k, vt, jnp.concatenate(wide, axis=1), m_own, qt_ref[...], s_ref, e_ref, exact
        )
        alpha = jnp.exp2((m_own - m) * EXP2_SCALE)
        o_ref[...] = o_own[...] * alpha + o
        stat_ref[0:1, :] = m
        stat_ref[1:2, :] = stat_own[1:2, :] * alpha + total
        totals.append(total)
        return totals

    @pl.when(exists(1))
    def _():
        twice(run)

    @pl.when(jnp.logical_not(exists(1)))
    def _():
        stat_ref[...] = stat_own[...]
        o_ref[...] = o_own[...]


def far_kernel(
    tok, heads, hops, n_kv, bias_ref, stat_own, o_near, stat_near, qt_ref, dot_ref, *refs
):
    pieces, refs = refs[:n_kv], refs[n_kv:]
    send_ref, keep_ref, ds_ref, attn_ref, stat_ref, k_ref, s_ref, e_ref, g_ref = refs
    tile = tile_of(tok)
    far = (hops - 1) * tok
    width = heads * tok
    wide = wide_blocks(tok, heads)

    def finish(cols, m, total, o):
        inverse = 1.0 / total
        attn = (o * inverse).astype(BF16)
        attn_ref[:, cols] = attn
        do_t = dot_ref[:, cols].astype(F32)
        delta = jnp.sum(do_t * attn.astype(F32), axis=0, keepdims=True)
        for row, other in ((0, stat_own), (1, stat_near)):
            stat_ref[row : row + 1, cols] = inverse * jnp.exp2(
                (other[0:1, cols] - m) * EXP2_SCALE
            )
        stat_ref[2:3, cols] = inverse
        stat_ref[3:4, cols] = delta
        return inverse, delta, do_t

    def run(exact):
        blocks = [gather_block(pieces[4 * d - 8 : 4 * d - 4]) for d in range(hops, 1, -1)]
        k = jnp.concatenate([b[0] for b in blocks], axis=0)
        v = jnp.concatenate([b[1] for b in blocks], axis=0)
        k_ref[...] = k
        k = beside_ones(k)
        vt = with_ones(v.T)
        dos, qs, totals = [], [], []
        for q0, cols in wide:
            bias = jnp.concatenate([bias_ref[q0:, q0 : q0 + tile]] * heads, axis=1)
            m_near = stat_near[0:1, cols]
            m, o, total = weights_of(
                k[q0:], vt[:, q0:], bias, m_near, qt_ref[:, cols],
                s_ref.at[q0:, cols], e_ref.at[q0:, cols], exact,
            )
            totals.append(total)
            alpha = jnp.exp2((m_near - m) * EXP2_SCALE)
            total = stat_near[1:2, cols] * alpha + total
            inverse, delta, do_t = finish(cols, m, total, o_near[:, cols] * alpha + o)
            dp = dot(v[q0:], dot_ref[:, cols], NN)
            ds_ref[q0:, cols] = e_ref[q0:, cols] * (dp - delta).astype(BF16)
            dos.append((do_t * inverse).astype(BF16))
            qs.append((qt_ref[:, cols].astype(F32) * (SCALE * inverse)).astype(BF16))
        dos, qs = jnp.concatenate(dos, axis=1), jnp.concatenate(qs, axis=1)
        for r0 in range(0, far, tile):
            rows = slice(r0, r0 + tile)
            c1 = min(width, (r0 // tile + 1) * heads * tile)
            g_ref[1, :, rows] = dot(dos[:, :c1], e_ref[rows, :c1], NT)
            g_ref[0, :, rows] = dot(qs[:, :c1], ds_ref[rows, :c1], NT)
        write_parts(send_ref, keep_ref, g_ref)
        return totals

    @pl.when(exists(2))
    def _():
        twice(run)

    @pl.when(jnp.logical_not(exists(2)))
    def _():
        send_ref[...] = jnp.zeros_like(send_ref)
        keep_ref[...] = jnp.zeros_like(keep_ref)
        for q0, cols in wide:
            finish(cols, stat_near[0:1, cols], stat_near[1:2, cols], o_near[:, cols])


def near_grad_kernel(
    tok, heads, e_ref, v_ref, stat_ref, qt_ref, dot_ref, send_ref, keep_ref, ds_ref, g_ref
):
    tile = tile_of(tok)

    @pl.when(exists(1))
    def _():
        inverse, delta = stat_ref[1:2, :], stat_ref[3:4, :]
        dp = dot(beside_ones(v_ref[...]), less(dot_ref[...], delta), NN)
        ds_ref[...] = e_ref[...] * dp.astype(BF16)
        dos = (dot_ref[...].astype(F32) * inverse).astype(BF16)
        qs = (qt_ref[...].astype(F32) * (SCALE * inverse)).astype(BF16)
        for which, left, right in ((1, dos, e_ref), (0, qs, ds_ref)):
            g_ref[which] = dot(left, right[...], NT)
            write_part(send_ref, keep_ref, g_ref, which)

    @pl.when(jnp.logical_not(exists(1)))
    def _():
        send_ref[...] = jnp.zeros_like(send_ref)
        keep_ref[...] = jnp.zeros_like(keep_ref)


def own_grad_kernel(
    tok, heads, e_ref, dp_ref, stat_ref, qt_ref, dot_ref, send_ref, keep_ref, ds_ref, g_ref
):
    tile = tile_of(tok)
    qs, dos = [], []
    for q0, h, c0 in col_blocks(tok, heads):
        cols = slice(c0, c0 + tile)
        rows = q0 + tile
        inverse, delta = stat_ref[0:1, cols], stat_ref[3:4, cols]
        ds_ref[0:rows, cols] = (
            e_ref[0:rows, cols].astype(F32) * (dp_ref[0:rows, cols] - delta)
        ).astype(BF16)
        dos.append((dot_ref[:, cols].astype(F32) * inverse).astype(BF16))
        qs.append((qt_ref[:, cols].astype(F32) * (SCALE * inverse)).astype(BF16))
    qs, dos = jnp.concatenate(qs, axis=1), jnp.concatenate(dos, axis=1)
    for r0 in range(0, tok, tile):
        rows, c0 = slice(r0, r0 + tile), r0 * heads
        g_ref[1, :, rows] = dot(dos[:, c0:], e_ref[rows, c0:], NT)
        g_ref[0, :, rows] = dot(qs[:, c0:], ds_ref[rows, c0:], NT)
    write_parts(send_ref, keep_ref, g_ref)


def query_kernel(
    tok, heads, hops, kt_own, k_near, k_far, ds_far, ds_near, ds_own, attn_ref, stat_ref,
    out_ref, qgrad_ref, sum_ref,
):
    tile = tile_of(tok)
    blocks = col_blocks(tok, heads)
    for q0, h, c0 in blocks:
        cols = slice(c0, c0 + tile)
        rows = q0 + tile
        out_ref[place_of(q0, h, tile)] = attn_ref[:, cols].T
        sum_ref[:, cols] = dot(kt_own[:, :rows], ds_own[0:rows, cols], NN) * stat_ref[0:1, cols]

    @pl.when(exists(1))
    def _():
        kt = k_near[...].T
        for q0, h, c0 in blocks:
            cols = slice(c0, c0 + tile)
            sum_ref[:, cols] += dot(kt, ds_near[:, cols], NN) * stat_ref[1:2, cols]

    @pl.when(exists(2))
    def _():
        kt = k_far[...].T
        for q0, h, c0 in blocks:
            cols = slice(c0, c0 + tile)
            sum_ref[:, cols] += dot(kt[:, q0:], ds_far[q0:, cols], NN) * stat_ref[2:3, cols]

    for q0, h, c0 in blocks:
        grad = sum_ref[:, c0 : c0 + tile] * SCALE
        qgrad_ref[place_of(q0, h, tile)] = grad.T.astype(BF16)


def sum_kernel(own_ref, *refs):
    for which, out_ref in enumerate(refs[-2:]):
        total = own_ref[0, which]
        for ref in refs[:-2]:
            total += ref[which].astype(F32)
        out_ref[...] = total


def call(kernel, shapes, operands, scratch=(), flops=0, limit=24):
    size = sum(math.prod(s.shape) * s.dtype.itemsize for s in shapes)
    size += sum(o.size * o.dtype.itemsize for o in operands)
    return pl.pallas_call(
        kernel,
        out_shape=shapes,
        in_specs=[pl.BlockSpec(memory_space=pltpu.VMEM)] * len(operands),
        out_specs=[pl.BlockSpec(memory_space=pltpu.VMEM)] * len(shapes),
        scratch_shapes=list(scratch),
        compiler_params=pltpu.CompilerParams(vmem_limit_bytes=limit << 20),
        cost_estimate=pl.CostEstimate(flops=flops, bytes_accessed=size, transcendentals=0),
    )(*operands)


def shift(array, step):
    size = lax.axis_size("ctx")
    route = [(c, c + step) for c in range(size) if 0 <= c + step < size]
    return lax.ppermute(array, "ctx", route)


def swap(array, stride):
    return lax.ppermute(array, "head", [(i, i ^ stride) for i in range(lax.axis_size("head"))])


def together(*arrays):
    return lax.optimization_barrier(arrays)


def body(queries, keys, values, out_grad, doc_start):
    tok, q_width = queries.shape
    heads = q_width // HEAD_DIM
    hops = WINDOW // tok
    reach = hops * tok
    far = reach - tok
    width = heads * tok
    part = HEAD_DIM // GROUP
    shape = jax.ShapeDtypeStruct
    everywhere = pl.BlockSpec(memory_space=pltpu.HBM)
    half, quarter = pl.pallas_call(
        pack_kernel,
        out_shape=[shape((tok, HEAD_DIM), BF16), shape((tok // 2, HEAD_DIM), BF16)],
        in_specs=[everywhere] * 2,
        out_specs=[pl.BlockSpec(memory_space=pltpu.VMEM)] * 2,
        scratch_shapes=[pltpu.SemaphoreType.DMA((2,))],
        compiler_params=pltpu.CompilerParams(vmem_limit_bytes=55040 << 10),
    )(keys, values)
    half = pl.pallas_call(
        late_pack_kernel,
        out_shape=shape((tok, HEAD_DIM), BF16),
        in_specs=[everywhere] * 2 + [pl.BlockSpec(memory_space=pltpu.VMEM)],
        out_specs=pl.BlockSpec(memory_space=pltpu.VMEM),
        scratch_shapes=[pltpu.SemaphoreType.DMA],
        input_output_aliases={2: 0},
        compiler_params=pltpu.CompilerParams(vmem_limit_bytes=55040 << 10),
    )(keys, values, half)
    came = [shift(quarter if d > 1 else half, d) for d in range(hops, 0, -1)][::-1]
    doc = doc_start.reshape(1, tok)
    causal = call(
        causal_kernel,
        [shape((tile_of(tok), tile_of(tok)), F32)],
        [],
        flops=64 * tok * tok * HEAD_DIM,
    )[0]
    causal, *tied = together(causal, *came[1:])
    came = [came[0], *tied]
    e_own, dp_own, o_own, stat_own, q_t, do_t, kt_own = call(
        functools.partial(own_kernel, tok, heads),
        [
            shape((tok, width), BF16),
            shape((tok, width), F32),
            shape((HEAD_DIM, width), F32),
            shape((2, width), F32),
            shape((HEAD_DIM, width), BF16),
            shape((HEAD_DIM, width), BF16),
            shape((HEAD_DIM, tok), BF16),
        ],
        [causal, doc, queries, keys, out_grad, values],
        scratch=[pltpu.VMEM((tok, width), F32)],
        flops=6 * tok * width * HEAD_DIM,
    )
    near, stat_own = together(came[0], stat_own)
    near = [near, swap(near, 1)]
    pieces = []
    for block in came[1:]:
        across = swap(block, 2)
        pieces += [block, across, swap(block, 1), swap(across, 1)]
    _, doc = together(stat_own, doc)
    near_bias, far_bias = call(
        functools.partial(mask_kernel, tok),
        [shape((tok, tok), F32), shape((far, tok), F32)],
        [doc],
        flops=64 * tok * tok * HEAD_DIM,
    )
    e_near, o_near, stat_near, k_near, v_near = call(
        functools.partial(near_kernel, tok, heads),
        [
            shape((tok, width), BF16),
            shape((HEAD_DIM, width), F32),
            shape((2, width), F32),
            shape((tok, HEAD_DIM), BF16),
            shape((tok, HEAD_DIM), BF16),
        ],
        [near_bias, o_own, stat_own, q_t, *near],
        scratch=[pltpu.VMEM((tok, width), F32)],
        flops=6 * tok * width * HEAD_DIM,
    )
    send_far, keep_far, ds_far, attn_t, stat, k_far = call(
        functools.partial(far_kernel, tok, heads, hops, len(pieces)),
        [
            shape((2, 2, part, far), BF16),
            shape((2, 2, part, far), F32),
            shape((far, width), BF16),
            shape((HEAD_DIM, width), BF16),
            shape((4, width), F32),
            shape((far, HEAD_DIM), BF16),
        ],
        [far_bias, stat_own, o_near, stat_near, q_t, do_t, *pieces],
        scratch=[
            pltpu.VMEM((far, width), F32),
            pltpu.VMEM((far, width), BF16),
            pltpu.VMEM((2, HEAD_DIM, far), F32),
        ],
        flops=10 * far * width * HEAD_DIM,
    )
    gradients = [
        shape((2, 2, part, tok), BF16),
        shape((2, 2, part, tok), F32),
        shape((tok, width), BF16),
    ]
    send_near, keep_near, ds_near = call(
        functools.partial(near_grad_kernel, tok, heads),
        gradients,
        [e_near, v_near, stat, q_t, do_t],
        scratch=[pltpu.VMEM((2, HEAD_DIM, tok), F32)],
        flops=6 * tok * width * HEAD_DIM,
    )
    pair_far = keep_far + swap(send_far, 1).astype(F32)
    whole = (pair_far[0] + swap(pair_far[1].astype(BF16), 2).astype(F32)).astype(BF16)
    pair_near = keep_near + swap(send_near, 1).astype(F32)
    pair_near, stat_late = together(pair_near, stat)
    near = (pair_near[0] + swap(pair_near[1].astype(BF16), 2).astype(F32)).astype(BF16)
    send_own, keep_own, ds_own = call(
        functools.partial(own_grad_kernel, tok, heads),
        gradients,
        [e_own, dp_own, stat_late, q_t, do_t],
        scratch=[pltpu.VMEM((2, HEAD_DIM, tok), F32)],
        flops=4 * tok * width * HEAD_DIM,
    )
    attn_out, query_grad = call(
        functools.partial(query_kernel, tok, heads, hops),
        [shape((tok, q_width), BF16)] * 2,
        [kt_own, k_near, k_far, ds_far, ds_near, ds_own, attn_t, stat],
        scratch=[pltpu.VMEM((HEAD_DIM, width), F32)],
        flops=2 * (reach + tok) * width * HEAD_DIM,
    )
    pair_own = keep_own + swap(send_own, 1).astype(F32)
    near, crossing = together(near, pair_own[1].astype(BF16))
    returned = [
        shift(whole[:, :, (hops - d) * tok : (hops - d + 1) * tok], -d) for d in range(hops, 1, -1)
    ]
    returned += [shift(near, -1), swap(crossing, 2)]
    key_grad, value_grad = call(
        sum_kernel, [shape((part, tok), F32)] * 2, [pair_own, *returned], limit=16
    )
    return attn_out, query_grad, key_grad.T, value_grad.T


def solution(mesh):
    placed = (P("ctx", "head"), P("ctx", None), P("ctx", None), P("ctx", "head"), P("ctx"))
    return jax.shard_map(
        body,
        mesh=mesh,
        in_specs=placed,
        out_specs=(P("ctx", "head"),) * 4,
        check_vma=False,
    )
```

time: 67.1 us -> 31.1 us (0.46)
  the two profiles are of different devices: /device:TPU:8 before, /device:TPU:0 now
where the time goes in v1:
time: 31.1 us; the launch traced here: 30.9 us
  starting transfers between devices  18 us (58%)
  waiting for transfers between devices  6.59 us (21%)
  Pallas kernels  5.16 us (17%)
  between operations  0.89 us (3%)
    ppermute x4, starting transfers between devices, shift(): return lax.ppermute(array, 'ctx', route)  11.2 us
    ppermute x10, starting transfers between devices, swap(): lax.ppermute(array, 'head', [(i, i ^ stride) for i in range(lax.axis_size...  6.85 us
    ppermute x10, waiting for transfers between devices, swap(): lax.ppermute(array, 'head', [(i, i ^ stride) for i in range(lax.axis_size...  4.34 us
    pallas_call x9, Pallas kernels, call(): pl.pallas_call(kernel, out_shape=shapes, in_specs=[pl.BlockSpec(memory_sp...  4.1 us
    ppermute x4, waiting for transfers between devices, shift(): return lax.ppermute(array, 'ctx', route)  2.25 us
    pallas_call x1, Pallas kernels, body(): pl.pallas_call(pack_kernel, out_shape=[shape((tok, HEAD_DIM), BF16), shap...  1.03 us
  transfers between devices with their start and end apart: 14, of which 6 were waited for; matrix products, arithmetic and copies ran while one was open for 1% of the time, Pallas kernels for 11%

profile of v1, /device:TPU:0, one launch (start us, length us, event | category | flops | bytes accessed | tf_op | source)
XLA Modules:
  0.0 30.9 jit_solution(3534719864299521766)
XLA Ops:
  0.6 1.0 %shard_map.85 = (bf16[512,128]{1,0:T(8,128)(2,1)S(1)}, bf16[256,128]{1,0:T(8,128)(2,1)S(1)}) custom-call(bf16[512,256]{1,0:T(8,128)(2,1)} %keys_hbm.3, bf16[512,256]{1,0:T(8,128)(2,1)} %values_hbm.3), custom_call_target="tpu_custom_call" | custom-call | tf_op jit(solution)/shard_map/pallas_call | solution.py:445
  1.7 5.0 %collective-permute-start = (bf16[256,128]{1,0:T(8,128)(2,1)S(1)}, bf16[256,128]{1,0:T(8,128)(2,1)S(1)}, u32[]{:S(2)}, u32[]{:S(2)}) collective-permute-start(bf16[256,128]{1,0:T(8,128)(2,1)S(1)} %get-tuple-element.45), channel_id=1, source_target_pairs={{0,16},{8,24},{1,17},{9,25},{2,18},{10,26},{3,19},{11,27},{4,20},{... | collective-permute-start | bytes 196616 | tf_op jit(solution)/shard_map/ppermute | solution.py:424
  6.7 0.0 copy-start
  6.7 0.0 copy-start.1
  6.7 0.0 copy-start.2
  6.7 0.0 copy-start.3
  6.7 0.0 copy-start.4
  6.7 3.6 %collective-permute-start.1 = (bf16[512,128]{1,0:T(8,128)(2,1)S(1)}, bf16[512,128]{1,0:T(8,128)(2,1)S(1)}, u32[]{:S(2)}, u32[]{:S(2)}) collective-permute-start(bf16[512,128]{1,0:T(8,128)(2,1)S(1)} %shard_map.87), channel_id=1, source_target_pairs={{0,8},{8,16},{16,24},{1,9},{9,17},{17,25},{2,10},{10,18},{18,26},{... | collective-permute-start | bytes 393224 | tf_op jit(solution)/shard_map/ppermute | solution.py:424
  10.4 0.0 collective-permute-done.refs_0_
  10.4 1.6 %collective-permute-start.3 = (bf16[256,128]{1,0:T(8,128)(2,1)S(1)}, bf16[256,128]{1,0:T(8,128)(2,1)S(1)}, u32[]{:S(2)}, u32[]{:S(2)}) collective-permute-start(bf16[256,128]{1,0:T(8,128)(2,1)S(1)} %collective-permute-done.refs_0_), channel_id=1, source_target_pairs={{0,2},{1,3},{2,0},{3,1},{4,6},{5,7},{6,4},{7,5},{8,10},{9,11},{10,... | collective-permute-start | bytes 196616 | tf_op jit(solution)/shard_map/ppermute | solution.py:428
  12.0 0.0 collective-permute-start.4
  12.0 0.0 copy-done
  12.0 0.0 copy-done.1
  12.0 0.0 copy-done.2
  12.0 0.0 copy-done.3
  12.0 0.0 copy-done.4
  12.0 1.2 %shard_map.86 = (bf16[512,1024]{1,0:T(8,128)(2,1)S(1)}, f32[512,1024]{1,0:T(8,128)S(1)}, f32[128,1024]{1,0:T(8,128)S(1)}, f32[2,1024]{1,0:T(2,128)S(1)}, bf16[12...) custom-call(f32[256,256]{1,0:T(8,128)S(1)} %shard_map.84.causal_ref, ...), custom_call_target="tpu_custom_call" | custom-call | flops 402653184 | bytes 5646336 | tf_op jit(solution)/shard_map/pallas_call | solution.py:410
  13.2 0.0 collective-permute-done.1.mine_ref
  13.2 0.6 %collective-permute-start.2 = (bf16[512,128]{1,0:T(8,128)(2,1)S(1)}, bf16[512,128]{1,0:T(8,128)(2,1)S(1)}, u32[]{:S(2)}, u32[]{:S(2)}) collective-permute-start(bf16[512,128]{1,0:T(8,128)(2,1)S(1)} %collective-permute-done.1.mine_ref), channel_id=1, source_target_pairs={{0,1},{1,0},{2,3},{3,2},{4,5},{5,4},{6,7},{7,6},{8,9},{9,8},{10,11... | collective-permute-start | bytes 393224 | tf_op jit(solution)/shard_map/ppermute | solution.py:428
  13.7 1.0 %collective-permute-done.3.refs_1_ = bf16[256,128]{1,0:T(8,128)(2,1)S(1)} collective-permute-done((bf16[256,128]{1,0:T(8,128)(2,1)S(1)}, bf16[256,128]{1,0:T(8,128)(2,1)S(1)}, u32[]{:S(2)}, u32[]{:S(2)}) %collective-permute-start.3) | collective-permute-done | bytes 65568 | tf_op jit(solution)/shard_map/ppermute | solution.py:428
  14.7 0.0 collective-permute-start.5
  14.7 0.2 shard_map.88
  14.9 0.0 collective-permute-done.2.other_ref
  14.9 0.1 shard_map.89
  15.0 0.0 collective-permute-done.4.refs_2_
  15.0 1.0 %collective-permute-done.5.refs_3_ = bf16[256,128]{1,0:T(8,128)(2,1)S(1)} collective-permute-done((bf16[256,128]{1,0:T(8,128)(2,1)S(1)}, bf16[256,128]{1,0:T(8,128)(2,1)S(1)}, u32[]{:S(2)}, u32[]{:S(2)}) %collective-permute-start.5) | collective-permute-done | bytes 65568 | tf_op jit(solution)/shard_map/ppermute | solution.py:428
  16.0 0.1 shard_map.90
  16.1 0.2 collective-permute-start.8
  16.4 0.4 %collective-permute-start.6 = (bf16[2,2,32,512]{3,2,1,0:T(8,128)(2,1)S(1)}, bf16[2,2,32,512]{3,2,1,0:T(8,128)(2,1)S(1)}, u32[]{:S(2)}, u32[]{:S(2)}) collective-permute-start(bf16[2,2,32,512]{3,2,1,0:T(8,128)(2,1)S(1)} %get-tuple-element.71), channel_id=1, source_target_pairs={{0,1},{1,0},{2,3},{3,2},{4,5},{5,4},{6,7},{7,6},{8,9},{9,8},{10,11... | collective-permute-start | bytes 393224 | tf_op jit(solution)/shard_map/ppermute | solution.py:428
  16.8 0.7 %collective-permute-done.8 = bf16[2,2,32,512]{3,2,1,0:T(8,128)(2,1)S(1)} collective-permute-done((bf16[2,2,32,512]{3,2,1,0:T(8,128)(2,1)S(1)}, bf16[2,2,32,512]{3,2,1,0:T(8,128)(2,1)S(1)}, u32[]{:S(2)}, u32[]{:S(2)}) %collective-permute-start.8) | collective-permute-done | bytes 131104 | tf_op jit(solution)/shard_map/ppermute | solution.py:428
  17.6 1.6 %collective-permute-start.9 = (bf16[2,32,512]{2,1,0:T(8,128)(2,1)S(1)}, bf16[2,32,512]{2,1,0:T(8,128)(2,1)S(1)}, u32[]{:S(2)}, u32[]{:S(2)}) collective-permute-start(bf16[2,32,512]{2,1,0:T(8,128)(2,1)S(1)} %fusion.3), channel_id=1, source_target_pairs={{0,2},{1,3},{2,0},{3,1},{4,6},{5,7},{6,4},{7,5},{8,10},{9,11},{10,... | collective-permute-start | bytes 196616 | tf_op jit(solution)/shard_map/ppermute | solution.py:428
  19.2 0.0 collective-permute-done.6
  19.2 0.6 %collective-permute-start.11 = (bf16[2,32,512]{2,1,0:T(8,128)(2,1)S(1)}, bf16[2,32,512]{2,1,0:T(8,128)(2,1)S(1)}, u32[]{:S(2)}, u32[]{:S(2)}) collective-permute-start(bf16[2,32,512]{2,1,0:T(8,128)(2,1)S(1)} %fusion.4), channel_id=1, source_target_pairs={{0,2},{1,3},{2,0},{3,1},{4,6},{5,7},{6,4},{7,5},{8,10},{9,11},{10,... | collective-permute-start | bytes 196616 | tf_op jit(solution)/shard_map/ppermute | solution.py:428
  19.8 0.7 %shard_map.92 = (bf16[2,2,32,512]{3,2,1,0:T(8,128)(2,1)S(1)}, f32[2,2,32,512]{3,2,1,0:T(8,128)S(1)}, bf16[512,1024]{1,0:T(8,128)(2,1)S(1)}) custom-call(bf16[512,1024]{1,0:T(8,128)(2,1)S(1)} %get-tuple-element.68.e_ref, f32[512,1024]{1,0:T(8,128)S(1)} %get-tuple-element.69.dp_ref, f32[4,1024]{1,0:T(4,128)S(1)} %get-tuple-element.72.stat_ref, ...), custom_call_target="tpu_custom_call" | custom-call | flops 268435456 | bytes 5128192 | tf_op jit(solution)/shard_map/pallas_call | solution.py:410
  20.6 0.1 collective-permute-start.7
  20.6 1.5 %collective-permute-done.9 = bf16[2,32,512]{2,1,0:T(8,128)(2,1)S(1)} collective-permute-done((bf16[2,32,512]{2,1,0:T(8,128)(2,1)S(1)}, bf16[2,32,512]{2,1,0:T(8,128)(2,1)S(1)}, u32[]{:S(2)}, u32[]{:S(2)}) %collective-permute-start.9) | collective-permute-done | bytes 65568 | tf_op jit(solution)/shard_map/ppermute | solution.py:428
  22.2 1.3 %collective-permute-start.10 = (bf16[2,32,512]{2,1,0:T(8,128)(2,1)S(1)}, bf16[2,32,512]{2,1,0:T(8,128)(2,1)S(1)}, u32[]{:S(2)}, u32[]{:S(2)}) collective-permute-start(bf16[2,32,512]{2,1,0:T(8,128)(2,1)S(1)} %fusion.1), channel_id=1, source_target_pairs={{16,0},{24,8},{17,1},{25,9},{18,2},{26,10},{19,3},{27,11},{20,4},{... | collective-permute-start | bytes 196616 | tf_op jit(solution)/shard_map/ppermute | solution.py:424
  23.5 0.1 collective-permute-done.11
  23.6 0.0 collective-permute-done.7
  23.6 1.3 %collective-permute-start.12 = (bf16[2,32,512]{2,1,0:T(8,128)(2,1)S(1)}, bf16[2,32,512]{2,1,0:T(8,128)(2,1)S(1)}, u32[]{:S(2)}, u32[]{:S(2)}) collective-permute-start(bf16[2,32,512]{2,1,0:T(8,128)(2,1)S(1)} %fusion.2), channel_id=1, source_target_pairs={{8,0},{16,8},{24,16},{9,1},{17,9},{25,17},{10,2},{18,10},{26,18},{... | collective-permute-start | bytes 196616 | tf_op jit(solution)/shard_map/ppermute | solution.py:424
  24.9 1.9 %collective-permute-start.13 = (bf16[2,32,512]{2,1,0:T(8,128)(2,1)S(1)}, bf16[2,32,512]{2,1,0:T(8,128)(2,1)S(1)}, u32[]{:S(2)}, u32[]{:S(2)}) collective-permute-start(bf16[2,32,512]{2,1,0:T(8,128)(2,1)S(1)} %fusion.5), channel_id=1, source_target_pairs={{0,2},{1,3},{2,0},{3,1},{4,6},{5,7},{6,4},{7,5},{8,10},{9,11},{10,... | collective-permute-start | bytes 196616 | tf_op jit(solution)/shard_map/ppermute | solution.py:428
  26.8 1.1 %shard_map.93 = (bf16[512,256]{1,0:T(8,128)(2,1)}, bf16[512,256]{1,0:T(8,128)(2,1)}) custom-call(bf16[128,512]{1,0:T(8,128)(2,1)S(1)} %get-tuple-element.47.kt_own, bf16[512,128]{1,0:T(8,128)(2,1)S(1)} %get-tuple-element.56.k_near, bf16[512,128]{1,0:T(8,128)(2,1)S(1)} %get-tuple-element.62.k_far, bf16[512,1024]{1,0:T(8,128)(2,1)S(1)} %get-tuple-element.63.ds_far, ...), custom_call_target="tpu_custom_call" | custom-call | flops 402653184 | bytes 4341760 | tf_op jit(solution)/shard_map/pallas_call | solution.py:410
  27.9 2.2 %collective-permute-done.10.refs_0_ = bf16[2,32,512]{2,1,0:T(8,128)(2,1)S(1)} collective-permute-done((bf16[2,32,512]{2,1,0:T(8,128)(2,1)S(1)}, bf16[2,32,512]{2,1,0:T(8,128)(2,1)S(1)}, u32[]{:S(2)}, u32[]{:S(2)}) %collective-permute-start.10) | collective-permute-done | bytes 65568 | tf_op jit(solution)/shard_map/ppermute | solution.py:424
  30.2 0.0 collective-permute-done.12.refs_1_
  30.2 0.0 collective-permute-done.13.refs_2_
  30.2 0.7 %shard_map.94 = (f32[32,512]{1,0:T(8,128)}, f32[32,512]{1,0:T(8,128)}) custom-call(f32[2,2,32,512]{3,2,1,0:T(8,128)S(1)} %convert_add_fusion.1.own_ref, bf16[2,32,512]{2,1,0:T(8,128)(2,1)S(1)} %collective-permute-done.10.refs_0_, bf16[2,32,512]{2,1,0:T(8,128)(2,1)S(1)} %collective-permute-done.12.refs_1_, bf16[2,32,512]{2,1,0:T(8,128)(2,1)S(1)} %collective-permute-done.13.refs_2_), custom_call_target="tpu_custom_call" | custom-call | bytes 589824 | tf_op jit(solution)/shard_map/pallas_call | solution.py:410
  (11 shorter events, 0.2 us)
Async XLA Ops:
  1.7 8.7 %collective-permute-start = (bf16[256,128]{1,0:T(8,128)(2,1)S(1)}, bf16[256,128]{1,0:T(8,128)(2,1)S(1)}, u32[]{:S(2)}, u32[]{:S(2)}) collective-permute-start(bf16[256,128]{1,0:T(8,128)(2,1)S(1)} %get-tuple-element.45), channel_id=1, source_target_pairs={{0,16},{8,24},{1,17},{9,25},{2,18},{10,26},{3,19},{11,27},{4,20},{... | collective-permute-start | bytes 196616 | tf_op jit(solution)/shard_map/ppermute | solution.py:424
  6.7 5.3 %copy-start = (bf16[512,256]{1,0:T(8,128)(2,1)S(1)}, bf16[512,256]{1,0:T(8,128)(2,1)}, u32[]{:S(2)}) copy-start(bf16[512,256]{1,0:T(8,128)(2,1)} %keys_hbm.3) | copy-start | bytes 786436
  6.7 5.3 %copy-start.1 = (bf16[512,256]{1,0:T(8,128)(2,1)S(1)}, bf16[512,256]{1,0:T(8,128)(2,1)}, u32[]{:S(2)}) copy-start(bf16[512,256]{1,0:T(8,128)(2,1)} %values_hbm.3) | copy-start | bytes 786436
  6.7 5.3 %copy-start.2 = (bf16[512,256]{1,0:T(8,128)(2,1)S(1)}, bf16[512,256]{1,0:T(8,128)(2,1)}, u32[]{:S(2)}) copy-start(bf16[512,256]{1,0:T(8,128)(2,1)} %q_ref.1) | copy-start | bytes 786436
  6.7 5.3 %copy-start.3 = (bf16[512,256]{1,0:T(8,128)(2,1)S(1)}, bf16[512,256]{1,0:T(8,128)(2,1)}, u32[]{:S(2)}) copy-start(bf16[512,256]{1,0:T(8,128)(2,1)} %do_ref.1) | copy-start | bytes 786436
  6.7 5.3 %copy-start.4 = (s32[512]{0:T(512)S(1)}, s32[512]{0:T(512)}, u32[]{:S(2)}) copy-start(s32[512]{0:T(512)} %param.9) | copy-start | bytes 6148
  6.7 6.4 %collective-permute-start.1 = (bf16[512,128]{1,0:T(8,128)(2,1)S(1)}, bf16[512,128]{1,0:T(8,128)(2,1)S(1)}, u32[]{:S(2)}, u32[]{:S(2)}) collective-permute-start(bf16[512,128]{1,0:T(8,128)(2,1)S(1)} %shard_map.87), channel_id=1, source_target_pairs={{0,8},{8,16},{16,24},{1,9},{9,17},{17,25},{2,10},{10,18},{18,26},{... | collective-permute-start | bytes 393224 | tf_op jit(solution)/shard_map/ppermute | solution.py:424
  10.4 4.3 %collective-permute-start.3 = (bf16[256,128]{1,0:T(8,128)(2,1)S(1)}, bf16[256,128]{1,0:T(8,128)(2,1)S(1)}, u32[]{:S(2)}, u32[]{:S(2)}) collective-permute-start(bf16[256,128]{1,0:T(8,128)(2,1)S(1)} %collective-permute-done.refs_0_), channel_id=1, source_target_pairs={{0,2},{1,3},{2,0},{3,1},{4,6},{5,7},{6,4},{7,5},{8,10},{9,11},{10,... | collective-permute-start | bytes 196616 | tf_op jit(solution)/shard_map/ppermute | solution.py:428
  12.0 3.0 %collective-permute-start.4 = (bf16[256,128]{1,0:T(8,128)(2,1)S(1)}, bf16[256,128]{1,0:T(8,128)(2,1)S(1)}, u32[]{:S(2)}, u32[]{:S(2)}) collective-permute-start(bf16[256,128]{1,0:T(8,128)(2,1)S(1)} %collective-permute-done.refs_0_), channel_id=1, source_target_pairs={{0,1},{1,0},{2,3},{3,2},{4,5},{5,4},{6,7},{7,6},{8,9},{9,8},{10,11... | collective-permute-start | bytes 196616 | tf_op jit(solution)/shard_map/ppermute | solution.py:428
  13.2 1.7 %collective-permute-start.2 = (bf16[512,128]{1,0:T(8,128)(2,1)S(1)}, bf16[512,128]{1,0:T(8,128)(2,1)S(1)}, u32[]{:S(2)}, u32[]{:S(2)}) collective-permute-start(bf16[512,128]{1,0:T(8,128)(2,1)S(1)} %collective-permute-done.1.mine_ref), channel_id=1, source_target_pairs={{0,1},{1,0},{2,3},{3,2},{4,5},{5,4},{6,7},{7,6},{8,9},{9,8},{10,11... | collective-permute-start | bytes 393224 | tf_op jit(solution)/shard_map/ppermute | solution.py:428
  14.7 1.3 %collective-permute-start.5 = (bf16[256,128]{1,0:T(8,128)(2,1)S(1)}, bf16[256,128]{1,0:T(8,128)(2,1)S(1)}, u32[]{:S(2)}, u32[]{:S(2)}) collective-permute-start(bf16[256,128]{1,0:T(8,128)(2,1)S(1)} %collective-permute-done.3.refs_1_), channel_id=1, source_target_pairs={{0,1},{1,0},{2,3},{3,2},{4,5},{5,4},{6,7},{7,6},{8,9},{9,8},{10,11... | collective-permute-start | bytes 196616 | tf_op jit(solution)/shard_map/ppermute | solution.py:428
  16.1 1.4 %collective-permute-start.8 = (bf16[2,2,32,512]{3,2,1,0:T(8,128)(2,1)S(1)}, bf16[2,2,32,512]{3,2,1,0:T(8,128)(2,1)S(1)}, u32[]{:S(2)}, u32[]{:S(2)}) collective-permute-start(bf16[2,2,32,512]{3,2,1,0:T(8,128)(2,1)S(1)} %get-tuple-element.80), channel_id=1, source_target_pairs={{0,1},{1,0},{2,3},{3,2},{4,5},{5,4},{6,7},{7,6},{8,9},{9,8},{10,11... | collective-permute-start | bytes 393224 | tf_op jit(solution)/shard_map/ppermute | solution.py:428
  16.4 2.8 %collective-permute-start.6 = (bf16[2,2,32,512]{3,2,1,0:T(8,128)(2,1)S(1)}, bf16[2,2,32,512]{3,2,1,0:T(8,128)(2,1)S(1)}, u32[]{:S(2)}, u32[]{:S(2)}) collective-permute-start(bf16[2,2,32,512]{3,2,1,0:T(8,128)(2,1)S(1)} %get-tuple-element.71), channel_id=1, source_target_pairs={{0,1},{1,0},{2,3},{3,2},{4,5},{5,4},{6,7},{7,6},{8,9},{9,8},{10,11... | collective-permute-start | bytes 393224 | tf_op jit(solution)/shard_map/ppermute | solution.py:428
  17.6 4.6 %collective-permute-start.9 = (bf16[2,32,512]{2,1,0:T(8,128)(2,1)S(1)}, bf16[2,32,512]{2,1,0:T(8,128)(2,1)S(1)}, u32[]{:S(2)}, u32[]{:S(2)}) collective-permute-start(bf16[2,32,512]{2,1,0:T(8,128)(2,1)S(1)} %fusion.3), channel_id=1, source_target_pairs={{0,2},{1,3},{2,0},{3,1},{4,6},{5,7},{6,4},{7,5},{8,10},{9,11},{10,... | collective-permute-start | bytes 196616 | tf_op jit(solution)/shard_map/ppermute | solution.py:428
  19.2 4.3 %collective-permute-start.11 = (bf16[2,32,512]{2,1,0:T(8,128)(2,1)S(1)}, bf16[2,32,512]{2,1,0:T(8,128)(2,1)S(1)}, u32[]{:S(2)}, u32[]{:S(2)}) collective-permute-start(bf16[2,32,512]{2,1,0:T(8,128)(2,1)S(1)} %fusion.4), channel_id=1, source_target_pairs={{0,2},{1,3},{2,0},{3,1},{4,6},{5,7},{6,4},{7,5},{8,10},{9,11},{10,... | collective-permute-start | bytes 196616 | tf_op jit(solution)/shard_map/ppermute | solution.py:428
  20.6 3.0 %collective-permute-start.7 = (bf16[2,2,32,512]{3,2,1,0:T(8,128)(2,1)S(1)}, bf16[2,2,32,512]{3,2,1,0:T(8,128)(2,1)S(1)}, u32[]{:S(2)}, u32[]{:S(2)}) collective-permute-start(bf16[2,2,32,512]{3,2,1,0:T(8,128)(2,1)S(1)} %get-tuple-element.78), channel_id=1, source_target_pairs={{0,1},{1,0},{2,3},{3,2},{4,5},{5,4},{6,7},{7,6},{8,9},{9,8},{10,11... | collective-permute-start | bytes 393224 | tf_op jit(solution)/shard_map/ppermute | solution.py:428
  22.2 8.0 %collective-permute-start.10 = (bf16[2,32,512]{2,1,0:T(8,128)(2,1)S(1)}, bf16[2,32,512]{2,1,0:T(8,128)(2,1)S(1)}, u32[]{:S(2)}, u32[]{:S(2)}) collective-permute-start(bf16[2,32,512]{2,1,0:T(8,128)(2,1)S(1)} %fusion.1), channel_id=1, source_target_pairs={{16,0},{24,8},{17,1},{25,9},{18,2},{26,10},{19,3},{27,11},{20,4},{... | collective-permute-start | bytes 196616 | tf_op jit(solution)/shard_map/ppermute | solution.py:424
  23.6 6.5 %collective-permute-start.12 = (bf16[2,32,512]{2,1,0:T(8,128)(2,1)S(1)}, bf16[2,32,512]{2,1,0:T(8,128)(2,1)S(1)}, u32[]{:S(2)}, u32[]{:S(2)}) collective-permute-start(bf16[2,32,512]{2,1,0:T(8,128)(2,1)S(1)} %fusion.2), channel_id=1, source_target_pairs={{8,0},{16,8},{24,16},{9,1},{17,9},{25,17},{10,2},{18,10},{26,18},{... | collective-permute-start | bytes 196616 | tf_op jit(solution)/shard_map/ppermute | solution.py:424
  24.9 5.2 %collective-permute-start.13 = (bf16[2,32,512]{2,1,0:T(8,128)(2,1)S(1)}, bf16[2,32,512]{2,1,0:T(8,128)(2,1)S(1)}, u32[]{:S(2)}, u32[]{:S(2)}) collective-permute-start(bf16[2,32,512]{2,1,0:T(8,128)(2,1)S(1)} %fusion.5), channel_id=1, source_target_pairs={{0,2},{1,3},{2,0},{3,1},{4,6},{5,7},{6,4},{7,5},{8,10},{9,11},{10,... | collective-permute-start | bytes 196616 | tf_op jit(solution)/shard_map/ppermute | solution.py:428
